TPU v7x, 1024 devices: a whole 4x8x16 slice. The times are simulated.
1024 devices in a mesh: dp: 16 (over y, core), expert: 64 (over z, x).
Axes of the slice: x: 4, y: 8, z: 16, core: 2. Of those that a mesh axis runs over, the one named last changes fastest.
Arguments:
- grad_out: bfloat16 [131072, 2048], P(('dp', 'expert')), may hold values from -6 to 6
- route_prob: bfloat16 [131072, 1], P(('dp', 'expert')), may hold values from 0.099609375 to 1
- expert_ids: int32 [131072, 1], P(('dp', 'expert')), may hold values from 0 to 63; in each aligned block of 128 rows (0 to 127, 128 to 255, ...) at most 3 rows name the same one
- saved_act: bfloat16 [16, 64, 192, 768], P('dp', 'expert'), may hold values from -0.21875 to 0.21875
- down_weight: bfloat16 [64, 768, 2048], P('expert'), may hold values from -0.21875 to 0.21875
Outputs:
- grad_act: bfloat16 [16, 64, 192, 768], P('dp', 'expert')
- grad_weight: float32 [64, 2048, 768], P('expert', 'dp')
- grad_prob: float32 [131072, 1], P(('dp', 'expert'))
Inputs may be any that keep to these rules, and one draw needn't show every extreme that they name: `expert_ids`: among the 128 tokens of one device no expert is named more than 3 times, a bound that some block reaches on every device.
All inputs are finite; a program needn't handle non-finite values.
Results may differ from a plain program's by a relative error of at most 0.0029.
Values may be sent and summed in bfloat16 or wider, within the bound.
A program may use at most 32 MiB of HBM per device.

v0:
```python
import jax
import jax.numpy as jnp
from jax import lax
from jax.sharding import PartitionSpec as P


def shards(grad_out, route_prob, expert_ids, saved_act, down_weight):
    expert_count = lax.axis_size("expert")
    slots = saved_act.shape[2]
    capacity = slots // expert_count
    width = grad_out.shape[1]
    routed = expert_ids[:, 0]
    member = (routed[:, None] == jnp.arange(expert_count, dtype=jnp.int32)[None, :]).astype(
        jnp.int32
    )
    before = jnp.cumsum(member, axis=0) - member
    placed = routed * capacity + jnp.sum(before * member, axis=1)
    send_rows = jnp.zeros((slots, width), jnp.bfloat16).at[placed].set(grad_out)
    send_prob = jnp.zeros((slots, 1), jnp.bfloat16).at[placed].set(route_prob)
    arrived, arrived_prob = (
        lax.all_to_all(send_rows, "expert", split_axis=0, concat_axis=0, tiled=True),
        lax.all_to_all(send_prob, "expert", split_axis=0, concat_axis=0, tiled=True),
    )
    stored = saved_act[0, 0]
    weight = down_weight[0]
    factor = arrived_prob.astype(jnp.float32)
    backed = lax.dot_general(
        arrived, weight, (((1,), (1,)), ((), ())), preferred_element_type=jnp.float32
    )
    grad_act = (factor * backed).astype(jnp.bfloat16)[None, None]
    slot_grad = jnp.sum(backed * stored.astype(jnp.float32), axis=1, keepdims=True)
    weighted = (factor * arrived.astype(jnp.float32)).astype(jnp.bfloat16)
    returned = lax.all_to_all(slot_grad, "expert", split_axis=0, concat_axis=0, tiled=True)
    grad_prob = returned[placed]
    grad_weight = lax.psum_scatter(
        lax.dot_general(
            weighted, stored, (((0,), (0,)), ((), ())), preferred_element_type=jnp.float32
        ),
        "dp",
        scatter_dimension=0,
        tiled=True,
    )
    return (grad_act, grad_weight[None], grad_prob)


def solution(mesh):
    return jax.shard_map(
        shards,
        mesh=mesh,
        in_specs=(
            P(("dp", "expert"), None),
            P(("dp", "expert"), None),
            P(("dp", "expert"), None),
            P("dp", "expert", None, None),
            P("expert", None, None),
        ),
        out_specs=(
            P("dp", "expert", None, None),
            P("expert", "dp", None),
            P(("dp", "expert"), None),
        ),
        check_vma=False,
    )
```

profile of v0, /device:TPU:1, one launch (start us, length us, event | category | flops | bytes accessed | tf_op | source)
XLA Modules:
  0.0 194.2 jit_solution(6916994387973566802)
XLA Ops:
  7.2 0.0 copy-start
  7.2 0.9 fusion.7
  8.1 0.2 reduce_window_sum.11
  8.2 0.8 select_reduce_fusion
  9.1 0.7 fusion.8
  9.7 1.5 scatter_custom_fusion
  11.2 0.8 all_to_all.30
  12.0 22.8 %all-to-all-start = ((bf16[64,3,1]{1,2,0:T(2,128)(2,1)}), bf16[64,3,1]{1,2,0:T(2,128)(2,1)S(1)}, u32[]{:S(2)}, u32[]{:S(2)}) async-start(bf16[64,3,1]{1,2,0:T(2,128)(2,1)} %all_to_all.30), calls=%async_computation | async-start | bytes 65536 | tf_op jit(solution)/shard_map/all_to_all | solution.py:22
  34.8 2.8 %scatter_custom_fusion.1 = bf16[192,2048]{1,0:T(8,128)(2,1)} fusion(s32[128]{0:T(128)S(1)} %fusion.8, bf16[128,2048]{1,0:T(8,128)(2,1)} %param.5, bf16[]{:T(256)} %constant.5.clone.1), kind=kCustom, calls=%fused_computation.8 | custom fusion | bytes 786944 | tf_op jit(solution)/shard_map/scatter | solution.py:18
  37.6 3.3 %all_to_all.24 = bf16[64,3,2048]{2,1,0:T(4,128)(2,1)} reshape(bf16[192,2048]{1,0:T(8,128)(2,1)} %scatter_custom_fusion.1) | data formatting | bytes 1572864 | tf_op jit(solution)/shard_map/all_to_all | solution.py:21
  40.9 0.0 copy-start.1
  40.9 7.2 %all-to-all-done = bf16[64,3,1]{1,2,0:T(2,128)(2,1)S(1)} async-done(((bf16[64,3,1]{1,2,0:T(2,128)(2,1)}), bf16[64,3,1]{1,2,0:T(2,128)(2,1)S(1)}, u32[]{:S(2)}, u32[]{:S(2)}) %all-to-all-start) | async-done | bytes 416 | tf_op jit(solution)/shard_map/all_to_all | solution.py:22
  48.2 7.7 %all-to-all-start.1 = ((bf16[64,3,2048]{2,1,0:T(4,128)(2,1)}), bf16[64,3,2048]{2,1,0:T(4,128)(2,1)}, u32[]{:S(2)}, u32[]{:S(2)}) async-start(bf16[64,3,2048]{2,1,0:T(4,128)(2,1)} %all_to_all.24), calls=%async_computation.1 | async-start | bytes 2097152 | tf_op jit(solution)/shard_map/all_to_all | solution.py:21
  55.9 0.0 reduce-scatter.2.cloned.1.call-start
  56.0 50.6 %all-to-all-done.1 = bf16[64,3,2048]{2,1,0:T(4,128)(2,1)} async-done(((bf16[64,3,2048]{2,1,0:T(4,128)(2,1)}), bf16[64,3,2048]{2,1,0:T(4,128)(2,1)}, u32[]{:S(2)}, u32[]{:S(2)}) %all-to-all-start.1) | async-done | bytes 786464 | tf_op jit(solution)/shard_map/all_to_all | solution.py:21
  106.6 2.7 %multiply_convert_fusion = bf16[64,3,2048]{2,1,0:T(4,128)(2,1)} fusion(bf16[64,3,2048]{2,1,0:T(4,128)(2,1)} %all-to-all-done.1, f32[64,3]{1,0:T(8,128)S(1)} %bitcast.28), kind=kLoop, calls=%fused_computation.5 | loop fusion | flops 1179648 | bytes 1573632 | tf_op jit(solution)/shard_map/convert_element_type | solution.py:32
  109.3 3.2 %convert_element_type.44 = bf16[192,2048]{1,0:T(8,128)(2,1)} reshape(bf16[64,3,2048]{2,1,0:T(4,128)(2,1)} %multiply_convert_fusion) | data formatting | bytes 1572864 | tf_op jit(solution)/shard_map/convert_element_type | solution.py:32
  112.5 0.0 copy-done.1
  112.5 4.8 %fusion.5 = f32[2048,768]{1,0:T(8,128)} fusion(bf16[192,2048]{1,0:T(8,128)(2,1)} %convert_element_type.44, bf16[1,1,192,768]{3,2,1,0:T(8,128)(2,1)S(1)} %copy-done.1), kind=kOutput, calls=%fused_computation.11 | convolution fusion | flops 603979776 | bytes 7372800 | tf_op jit(solution)/shard_map/dot_general | solution.py:36
  117.3 0.0 reduce-scatter.2.cloned.1.call-update
  117.3 0.1 convert_reduce_fusion
  117.4 0.1 reshape.32
  117.5 3.2 %all_to_all.26 = bf16[192,2048]{1,0:T(8,128)(2,1)} reshape(bf16[64,3,2048]{2,1,0:T(4,128)(2,1)} %all-to-all-done.1) | data formatting | bytes 1572864 | tf_op jit(solution)/shard_map/all_to_all | solution.py:21
  120.7 0.0 copy-done
  120.7 3.2 %multiply_reduce_fusion = (f32[192]{0:T(256)S(1)}, bf16[1,1,192,768]{3,2,1,0:T(8,128)(2,1)}) fusion(bf16[1,1,192,768]{3,2,1,0:T(8,128)(2,1)S(1)} %copy-done.1, f32[192]{0:T(256)S(1)} %reshape.32, bf16[192,2048]{1,0:T(8,128)(2,1)} %all_to_all.26, bf16[1,768,2048]{2,1,0:T(8,128)(2,1)S(1)} %copy-done), kind=kOutput, calls=%fused_computation.6 | convolution fusion | flops 604716864 | bytes 4523520 | tf_op jit(solution)/shard_map/dot_general | solution.py:27
  123.9 0.7 all_to_all.27
  124.6 8.7 %all-to-all-start.2 = ((f32[64,3,1]{1,2,0:T(1,128)}), f32[64,3,1]{1,2,0:T(1,128)S(1)}, u32[]{:S(2)}, u32[]{:S(2)}) async-start(f32[64,3,1]{1,2,0:T(1,128)} %bitcast.9), calls=%async_computation.3 | async-start | bytes 65536 | tf_op jit(solution)/shard_map/all_to_all | solution.py:33
  133.4 13.4 %all-to-all-done.2 = f32[64,3,1]{1,2,0:T(1,128)S(1)} async-done(((f32[64,3,1]{1,2,0:T(1,128)}), f32[64,3,1]{1,2,0:T(1,128)S(1)}, u32[]{:S(2)}, u32[]{:S(2)}) %all-to-all-start.2) | async-done | bytes 800 | tf_op jit(solution)/shard_map/all_to_all | solution.py:33
  146.8 0.5 broadcast.34
  147.3 0.7 reduce.7
  148.1 0.1 reshape.34
  148.2 1.8 gather_fusion
  150.0 37.4 %reduce-scatter.2.cloned.1.call-done = f32[128,768]{1,0:T(8,128)} async-done(((f32[2048,768]{1,0:T(8,128)}), f32[128,768]{1,0:T(8,128)}) %reduce-scatter.2.cloned.1.call-update) | async-done | bytes 393232 | tf_op jit(solution)/shard_map/reduce_scatter | solution.py:35
  (2 shorter events, 0.0 us)
Async XLA Ops:
  7.2 113.6 %copy-start = (bf16[1,768,2048]{2,1,0:T(8,128)(2,1)S(1)}, bf16[1,768,2048]{2,1,0:T(8,128)(2,1)}, u32[]{:S(2)}) copy-start(bf16[1,768,2048]{2,1,0:T(8,128)(2,1)} %param.9) | copy-start | bytes 9437188
  12.0 36.2 %all-to-all-start = ((bf16[64,3,1]{1,2,0:T(2,128)(2,1)}), bf16[64,3,1]{1,2,0:T(2,128)(2,1)S(1)}, u32[]{:S(2)}, u32[]{:S(2)}) async-start(bf16[64,3,1]{1,2,0:T(2,128)(2,1)} %all_to_all.30), calls=%async_computation | async-start | bytes 65536 | tf_op jit(solution)/shard_map/all_to_all | solution.py:22
  40.9 71.5 %copy-start.1 = (bf16[1,1,192,768]{3,2,1,0:T(8,128)(2,1)S(1)}, bf16[1,1,192,768]{3,2,1,0:T(8,128)(2,1)}, u32[]{:S(2)}) copy-start(bf16[1,1,192,768]{3,2,1,0:T(8,128)(2,1)} %param.8) | copy-start | bytes 884740
  48.2 58.4 %all-to-all-start.1 = ((bf16[64,3,2048]{2,1,0:T(4,128)(2,1)}), bf16[64,3,2048]{2,1,0:T(4,128)(2,1)}, u32[]{:S(2)}, u32[]{:S(2)}) async-start(bf16[64,3,2048]{2,1,0:T(4,128)(2,1)} %all_to_all.24), calls=%async_computation.1 | async-start | bytes 2097152 | tf_op jit(solution)/shard_map/all_to_all | solution.py:21
  55.9 131.5 %reduce-scatter.2.cloned.1.call-start = ((), (), s32[]{:S(2)}) async-start(), calls=%async_computation.4 | async-start | bytes 6684672 | tf_op jit(solution)/shard_map/reduce_scatter | solution.py:35
  124.6 22.2 %all-to-all-start.2 = ((f32[64,3,1]{1,2,0:T(1,128)}), f32[64,3,1]{1,2,0:T(1,128)S(1)}, u32[]{:S(2)}, u32[]{:S(2)}) async-start(f32[64,3,1]{1,2,0:T(1,128)} %bitcast.9), calls=%async_computation.3 | async-start | bytes 65536 | tf_op jit(solution)/shard_map/all_to_all | solution.py:33
Sparse Core Ops, SparseCore 0:
  117.4 69.9 reduce-scatter.1
where the time goes:
time: 195 us; the launch traced here: 194 us
  waiting for transfers between devices  109 us (56%)
  starting transfers between devices  39.2 us (20%)
  local copies, waits for them, and re-layouts  18.1 us (9%)
  between operations  14.1 us (7%)
  matrix products  7.99 us (4%)
  other arithmetic  6.11 us (3%)
    all_to_all x1, waiting for transfers between devices, shards(): lax.all_to_all(send_rows, 'expert', split_axis=0, concat_axis=0, tiled=True)  50.6 us
    reduce_scatter x1, waiting for transfers between devices, shards(): lax.psum_scatter(lax.dot_general(weighted, stored, (((0,), (0,)), ((), ()...  37.4 us
    all_to_all x1, starting transfers between devices, shards(): lax.all_to_all(send_prob, 'expert', split_axis=0, concat_axis=0, tiled=True)  22.8 us
    all_to_all x1, waiting for transfers between devices, shards(): lax.all_to_all(slot_grad, 'expert', split_axis=0, concat_axis=0, tiled=True)  13.4 us
    all_to_all x1, starting transfers between devices, shards(): lax.all_to_all(slot_grad, 'expert', split_axis=0, concat_axis=0, tiled=True)  8.71 us
    all_to_all x1, starting transfers between devices, shards(): lax.all_to_all(send_rows, 'expert', split_axis=0, concat_axis=0, tiled=True)  7.68 us
    all_to_all x1, waiting for transfers between devices, shards(): lax.all_to_all(send_prob, 'expert', split_axis=0, concat_axis=0, tiled=True)  7.24 us
    all_to_all x2, local copies, waits for them, and re-layouts, shards(): lax.all_to_all(send_rows, 'expert', split_axis=0, concat_axis=0, tiled=True)  6.48 us
  transfers between devices with their start and end apart: 4, of which 4 were waited for; matrix products, arithmetic and copies ran while one was open for 5% of the time, Pallas kernels for 0%

commit v1 on v0

v1 whole, which is shorter than its diff:
```python
import functools

import jax
import jax.numpy as jnp
from jax import lax
from jax.experimental import pallas as pl
from jax.experimental.pallas import tpu as pltpu
from jax.sharding import PartitionSpec as P

MESH = pl.DeviceIdType.MESH
NZ, NX = 16, 4
NE = NZ * NX
NDP = 16
CAP = 3
CHUNKS = 4
PEERS = NE // CHUNKS
ROWS = PEERS * CAP
SLOTS = NE * CAP
SELF = NE - NX
TOK = 128
WIDTH = 2048
FFW = 768
PIECES = WIDTH // 128
F32 = jnp.float32
BF16 = jnp.bfloat16


def offset_of(o):
    q = o // NX
    half = (q + 1) // 2
    return NZ // 2 + half * (1 - 2 * (q % 2)), o % NX


def target_of(o, z, x):
    dz, dx = offset_of(o)
    return ((z + dz) % NZ) * NX + (x + dx) % NX


def source_of(o, z, x):
    dz, dx = offset_of(o)
    return ((z + NZ - dz) % NZ) * NX + (x + NX - dx) % NX


def slot_parts(slot):
    chunk = (
        (slot >= ROWS).astype(jnp.int32)
        + (slot >= 2 * ROWS).astype(jnp.int32)
        + (slot >= 3 * ROWS).astype(jnp.int32)
    )
    rest = slot - ROWS * chunk
    return PEERS * chunk + rest % PEERS, rest // PEERS


def dot(a, b):
    return lax.dot_general(a, b, (((1,), (0,)), ((), ())), preferred_element_type=F32)


def kernel(
    ids_ref, prob_ref, grad_hbm, saved_hbm, weight_hbm,
    act_ref, gw_ref, gp_ref,
    grad, saved, weight, onehot, swap, to_natural,
    send, recv, psend, precv, gsend, grecv,
    arrived, act, wsend, wrecv, gathered,
    load_sem, tok_send, tok_recv, p_send, p_recv, g_send, g_recv,
    w_send, w_recv, s_send, right_recv, left_recv, twin_recv,
):
    dp, me = lax.axis_index("dp"), lax.axis_index("expert")
    z, x = me // NX, me % NX
    y, core = dp // 2, dp % 2
    twin = dp + 1 - 2 * core
    right, left = (dp + 2) % NDP, (dp + NDP - 2) % NDP

    barrier = pltpu.get_barrier_semaphore()

    @pl.loop(0, NE)
    def _(o):
        @pl.when(o != SELF)
        def _():
            pl.semaphore_signal(
                barrier, inc=1, device_id=(dp, target_of(o, z, x)), device_id_type=MESH
            )

    @pl.loop(1, NDP)
    def _(i):
        pl.semaphore_signal(
            barrier, inc=1, device_id=((dp + i) % NDP, me), device_id_type=MESH
        )

    loads = [
        pltpu.make_async_copy(grad_hbm, grad, load_sem.at[0]),
        pltpu.make_async_copy(saved_hbm, saved, load_sem.at[1]),
        pltpu.make_async_copy(weight_hbm, weight, load_sem.at[2]),
    ]
    for load in loads:
        load.start()

    ids = jnp.broadcast_to(ids_ref[...], (TOK, TOK)).astype(F32)
    earlier = lax.broadcasted_iota(jnp.int32, (TOK, TOK), 0) < lax.broadcasted_iota(
        jnp.int32, (TOK, TOK), 1
    )
    same = jnp.where(earlier & (ids.T == ids), 1.0, 0.0)
    before = jnp.sum(same, axis=0, keepdims=True)
    peer, k = slot_parts(lax.broadcasted_iota(jnp.int32, (SLOTS, TOK), 0))
    onehot[...] = jnp.where(
        (target_of(peer, z, x) == ids_ref[...]) & (k.astype(F32) == before), 1.0, 0.0
    )
    lane = lax.broadcasted_iota(jnp.int32, (PEERS, 128), 1)

    def by_lane(column):
        out = jnp.zeros((PEERS, 128), F32)
        for i in range(CAP):
            out = jnp.where(lane == i, column[PEERS * i : PEERS * (i + 1)], out)
        return out

    probs = jnp.sum(onehot[...] * prob_ref[...].astype(F32), axis=1, keepdims=True)
    for j in range(CHUNKS):
        psend[PEERS * j : PEERS * (j + 1), 0, :] = by_lane(probs[ROWS * j : ROWS * (j + 1)])

    row = lax.broadcasted_iota(jnp.int32, (256, 256), 0)
    col = lax.broadcasted_iota(jnp.int32, (256, 256), 1)
    swap[...] = jnp.where(col == 16 * (row % 16) + row // 16, 1.0, 0.0).astype(BF16)

    loads[0].wait()
    for j in range(CHUNKS):
        picked = dot(onehot[ROWS * j : ROWS * (j + 1), :].astype(BF16), grad[...]).astype(BF16)
        for i in range(CAP):
            tiles = jnp.concatenate(
                [picked[PEERS * i : PEERS * (i + 1), 128 * c : 128 * (c + 1)] for c in range(PIECES)],
                axis=0,
            )
            out = dot(swap[...], tiles).astype(BF16).reshape(PEERS, PIECES, 128)
            send[PEERS * j : PEERS * (j + 1), PIECES * i : PIECES * (i + 1), :] = out
        if j == 0:
            pl.semaphore_wait(barrier, NE - 1 + NDP - 1)

        @pl.loop(PEERS * j, min(PEERS * (j + 1), NE))
        def _(o):
            @pl.when(o != SELF)
            def _():
                peer_id = (dp, target_of(o, z, x))
                pltpu.make_async_remote_copy(
                    src_ref=send.at[o], dst_ref=recv.at[o],
                    send_sem=tok_send, recv_sem=tok_recv.at[j],
                    device_id=peer_id, device_id_type=MESH,
                ).start()
                pltpu.make_async_remote_copy(
                    src_ref=psend.at[o], dst_ref=precv.at[o],
                    send_sem=p_send, recv_sem=p_recv.at[j],
                    device_id=peer_id, device_id_type=MESH,
                ).start()

    recv[SELF] = send[SELF]
    precv[SELF] = psend[SELF]

    slot_r = lax.broadcasted_iota(jnp.int32, (SLOTS, SLOTS), 0)
    slot_c = lax.broadcasted_iota(jnp.int32, (SLOTS, SLOTS), 1)
    peer_r, k_r = slot_parts(slot_r)
    to_chunk = jnp.where(source_of(peer_r, z, x) * CAP + k_r == slot_c, 1.0, 0.0).astype(BF16)
    peer_c, k_c = slot_parts(slot_c)
    to_natural[...] = jnp.where(
        source_of(peer_c, z, x) * CAP + k_c == slot_r, 1.0, 0.0
    ).astype(BF16)
    loads[1].wait()
    own = dot(to_chunk, saved[...]).astype(BF16)
    for j in range(CHUNKS):
        gathered[j, dp] = own[ROWS * j : ROWS * (j + 1)]

    def pass_on(j, r, device, sem):
        pltpu.make_async_remote_copy(
            src_ref=gathered.at[j, r], dst_ref=gathered.at[j, r],
            send_sem=s_send, recv_sem=sem,
            device_id=(device, me), device_id_type=MESH,
        ).start()

    def await_piece(j, r, sem):
        pltpu.make_async_remote_copy(
            src_ref=gathered.at[j, r], dst_ref=gathered.at[j, r],
            send_sem=s_send, recv_sem=sem,
            device_id=(twin, me), device_id_type=MESH,
        ).wait_recv()

    for j in range(CHUNKS):
        pass_on(j, dp, right, right_recv.at[0, j])
        pass_on(j, dp, left, left_recv.at[0, j])
    for j in range(CHUNKS):
        pass_on(j, dp, twin, twin_recv)
    for hop in range(1, 5):
        from_left, from_right = (dp + NDP - 2 * hop) % NDP, (dp + 2 * hop) % NDP
        for j in range(CHUNKS):
            if hop < 4 or j < 2:
                await_piece(j, from_left, right_recv.at[hop - 1, j])
                if hop < 3 or (hop == 3 and j < 2):
                    pass_on(j, from_left, right, right_recv.at[hop, j])
                pass_on(j, from_left, twin, twin_recv)
            if hop < 4 or j >= 2:
                await_piece(j, from_right, left_recv.at[hop - 1, j])
                if hop < 3 or (hop == 3 and j >= 2):
                    pass_on(j, from_right, left, left_recv.at[hop, j])
                pass_on(j, from_right, twin, twin_recv)
    loads[2].wait()

    def take(j):
        count = PEERS - (1 if j == CHUNKS - 1 else 0)
        pltpu.make_async_remote_copy(
            src_ref=send.at[pl.ds(0, count)], dst_ref=recv.at[pl.ds(0, count)],
            send_sem=tok_send, recv_sem=tok_recv.at[j],
            device_id=(dp, me), device_id_type=MESH,
        ).wait_recv()
        pltpu.make_async_remote_copy(
            src_ref=psend.at[pl.ds(0, count)], dst_ref=precv.at[pl.ds(0, count)],
            send_sem=p_send, recv_sem=p_recv.at[j],
            device_id=(dp, me), device_id_type=MESH,
        ).wait_recv()
        factor = precv[PEERS * j : PEERS * (j + 1), 0, :]
        for i in range(CAP):
            tiles = recv[PEERS * j : PEERS * (j + 1), PIECES * i : PIECES * (i + 1), :]
            turned = dot(swap[...], tiles.reshape(PEERS * PIECES, 128))
            part = jnp.broadcast_to(factor[:, i : i + 1], (PEERS, 128))
            at = ROWS * j + PEERS * i
            for c in range(PIECES):
                tile = turned[PEERS * c : PEERS * (c + 1)]
                arrived[at : at + PEERS, 128 * c : 128 * (c + 1)] = tile.astype(BF16)
                wsend[j, c, PEERS * i : PEERS * (i + 1), :] = (tile * part).astype(BF16)
        wrecv[j, dp] = wsend[j, dp]

        @pl.loop(1, NDP)
        def _(i):
            to = (dp + i) % NDP
            pltpu.make_async_remote_copy(
                src_ref=wsend.at[j, to], dst_ref=wrecv.at[j, dp],
                send_sem=w_send, recv_sem=w_recv.at[j],
                device_id=(to, me), device_id_type=MESH,
            ).start()

    def back(j):
        rows = slice(ROWS * j, ROWS * (j + 1))
        backed = lax.dot_general(
            arrived[rows, :], weight[...], (((1,), (1,)), ((), ())), preferred_element_type=F32
        )
        mine = gathered[j, dp].astype(F32)
        gsend[PEERS * j : PEERS * (j + 1), 0, :] = by_lane(
            jnp.sum(backed * mine, axis=1, keepdims=True)
        )

        @pl.loop(PEERS * j, PEERS * (j + 1))
        def _(o):
            @pl.when(o != SELF)
            def _():
                pltpu.make_async_remote_copy(
                    src_ref=gsend.at[o], dst_ref=grecv.at[o],
                    send_sem=g_send, recv_sem=g_recv,
                    device_id=(dp, source_of(o, z, x)), device_id_type=MESH,
                ).start()

        factor = precv[PEERS * j : PEERS * (j + 1), 0, :]
        for i in range(CAP):
            part = jnp.broadcast_to(factor[:, i : i + 1], (PEERS, FFW))
            at = PEERS * i
            act[ROWS * j + at : ROWS * j + at + PEERS, :] = (
                part * backed[at : at + PEERS]
            ).astype(BF16)

    def add(j):
        pltpu.make_async_remote_copy(
            src_ref=wsend.at[j, pl.ds(0, NDP - 1)], dst_ref=wrecv.at[j, pl.ds(0, NDP - 1)],
            send_sem=w_send, recv_sem=w_recv.at[j],
            device_id=(dp, me), device_id_type=MESH,
        ).wait_recv()
        part = lax.dot_general(
            wrecv[j].reshape(NDP * ROWS, 128), gathered[j].reshape(NDP * ROWS, FFW),
            (((0,), (0,)), ((), ())), preferred_element_type=F32,
        )
        if j == 0:
            gw_ref[...] = part
        else:
            gw_ref[...] += part

    take(0)
    back(0)
    take(1)
    back(1)
    pltpu.make_async_remote_copy(
        src_ref=gathered.at[:, pl.ds(0, NDP // 2)], dst_ref=gathered.at[:, pl.ds(0, NDP // 2)],
        send_sem=s_send, recv_sem=twin_recv, device_id=(twin, me), device_id_type=MESH,
    ).wait_recv()
    take(2)
    take(3)
    back(2)
    back(3)
    grecv[SELF] = gsend[SELF]
    add(0)
    add(1)
    act_ref[...] = dot(to_natural[...], act[...]).astype(BF16)
    add(2)
    add(3)

    def all_but_one(ref, sem):
        return pltpu.make_async_remote_copy(
            src_ref=ref.at[pl.ds(0, NE - 1)], dst_ref=ref.at[pl.ds(0, NE - 1)],
            send_sem=sem, recv_sem=g_recv, device_id=(dp, me), device_id_type=MESH,
        )

    all_but_one(grecv, g_send).wait_recv()
    total = jnp.zeros((PEERS, TOK), F32)
    for j in range(CHUNKS):
        back_sum = grecv[PEERS * j : PEERS * (j + 1), 0, :]
        for i in range(CAP):
            at = ROWS * j + PEERS * i
            total += onehot[at : at + PEERS, :] * jnp.broadcast_to(
                back_sum[:, i : i + 1], (PEERS, TOK)
            )
    gp_ref[...] = jnp.sum(total, axis=0, keepdims=True)

    all_but_one(send, tok_send).wait_send()
    all_but_one(psend, p_send).wait_send()
    all_but_one(gsend, g_send).wait_send()
    pltpu.make_async_remote_copy(
        src_ref=wsend.at[:, pl.ds(0, NDP - 1)], dst_ref=wsend.at[:, pl.ds(0, NDP - 1)],
        send_sem=w_send, recv_sem=g_recv, device_id=(dp, me), device_id_type=MESH,
    ).wait_send()
    pltpu.make_async_remote_copy(
        src_ref=gathered.at[:, pl.ds(0, NDP - 1)], dst_ref=gathered.at[:, pl.ds(0, NDP - 1)],
        send_sem=s_send, recv_sem=g_recv, device_id=(dp, me), device_id_type=MESH,
    ).wait_send()


def shards(grad_out, route_prob, expert_ids, saved_act, down_weight):
    vmem = pl.BlockSpec(memory_space=pltpu.VMEM)
    anywhere = pl.BlockSpec(memory_space=pl.ANY)
    dma = pltpu.SemaphoreType.DMA
    act, grad_weight, grad_prob = pl.pallas_call(
        kernel,
        out_shape=[
            jax.ShapeDtypeStruct((SLOTS, FFW), BF16),
            jax.ShapeDtypeStruct((128, FFW), F32),
            jax.ShapeDtypeStruct((1, TOK), F32),
        ],
        in_specs=[vmem, vmem, anywhere, anywhere, anywhere],
        out_specs=[vmem, vmem, vmem],
        scratch_shapes=[
            pltpu.VMEM((TOK, WIDTH), BF16),
            pltpu.VMEM((SLOTS, FFW), BF16),
            pltpu.VMEM((FFW, WIDTH), BF16),
            pltpu.VMEM((SLOTS, TOK), F32),
            pltpu.VMEM((256, 256), BF16),
            pltpu.VMEM((SLOTS, SLOTS), BF16),
            pltpu.VMEM((NE, CAP * PIECES, 128), BF16),
            pltpu.VMEM((NE, CAP * PIECES, 128), BF16),
            pltpu.VMEM((NE, 1, 128), F32),
            pltpu.VMEM((NE, 1, 128), F32),
            pltpu.VMEM((NE, 1, 128), F32),
            pltpu.VMEM((NE, 1, 128), F32),
            pltpu.VMEM((SLOTS, WIDTH), BF16),
            pltpu.VMEM((SLOTS, FFW), BF16),
            pltpu.VMEM((CHUNKS, NDP, ROWS, 128), BF16),
            pltpu.VMEM((CHUNKS, NDP, ROWS, 128), BF16),
            pltpu.VMEM((CHUNKS, NDP, ROWS, FFW), BF16),
            dma((3,)),
            dma, dma((CHUNKS,)),
            dma, dma((CHUNKS,)),
            dma, dma,
            dma, dma((CHUNKS,)),
            dma, dma((4, CHUNKS)), dma((4, CHUNKS)), dma,
        ],
        compiler_params=pltpu.CompilerParams(
            collective_id=0, has_side_effects=True, vmem_limit_bytes=40 << 20
        ),
        cost_estimate=pl.CostEstimate(
            flops=2_000_000_000, bytes_accessed=6_000_000, transcendentals=0
        ),
    )(
        expert_ids.reshape(1, TOK), route_prob.reshape(1, TOK), grad_out,
        saved_act.reshape(SLOTS, FFW), down_weight.reshape(FFW, WIDTH),
    )
    return act[None, None], grad_weight[None], grad_prob.reshape(TOK, 1)


def solution(mesh):
    return jax.shard_map(
        shards,
        mesh=mesh,
        in_specs=(
            P(("dp", "expert"), None),
            P(("dp", "expert"), None),
            P(("dp", "expert"), None),
            P("dp", "expert", None, None),
            P("expert", None, None),
        ),
        out_specs=(
            P("dp", "expert", None, None),
            P("expert", "dp", None),
            P(("dp", "expert"), None),
        ),
        check_vma=False,
    )
```

time: 195 us -> 83.3 us (0.43)
  waiting for transfers between devices: 109 us -> 0 us
  Pallas kernels: 0 us -> 75.2 us
  starting transfers between devices: 39.2 us -> 0 us
  between operations: 14.1 us -> 0.65 us
  local copies, waits for them, and re-layouts: 18.1 us -> 7.17 us
  matrix products: 7.99 us -> 0 us
  other arithmetic: 6.11 us -> 0 us
    pallas_call x0 -> x1, Pallas kernels: none -> 75.2 us  [shards(): pl.pallas_call(kernel, out_shape=[jax.ShapeDtypeStruct((SLOTS, FFW), BF16...]
    all_to_all x3 -> x0, waiting for transfers between devices: 71.3 us -> none  [the longest x1 50.6 us: shards(): lax.all_to_all(send_rows, 'expert', split_axis=0, concat_axis=0, tiled=True)]
    all_to_all x3 -> x0, starting transfers between devices: 39.2 us -> none  [the longest x1 22.8 us: shards(): lax.all_to_all(send_prob, 'expert', split_axis=0, concat_axis=0, tiled=True)]
    reduce_scatter x1 -> x0, waiting for transfers between devices: 37.4 us -> none  [shards(): lax.psum_scatter(lax.dot_general(weighted, stored, (((0,), (0,)), ((), ()...]
    all_to_all x6 -> x0, local copies, waits for them, and re-layouts: 8.64 us -> none  [the longest x2 6.48 us: shards(): lax.all_to_all(send_rows, 'expert', split_axis=0, concat_axis=0, tiled=True)]
    dot_general x2 -> x0, matrix products: 7.99 us -> none  [the longest x1 4.83 us: shards(): lax.dot_general(weighted, stored, (((0,), (0,)), ((), ())), preferred_ele...]
    unnamed x4 -> x13, local copies, waits for them, and re-layouts: 0.01 us -> 7.17 us
    scatter x2 -> x0, local copies, waits for them, and re-layouts: 4.32 us -> none  [the longest x1 2.84 us: shards(): send_rows = jnp.zeros((slots, width), jnp.bfloat16).at[placed].set(grad_out)]
  transfers between devices with their start and end apart: 4 -> 0, of which waited for: 4 -> 0; matrix products, arithmetic and copies ran while one was open for 5% -> 0% of each run, Pallas kernels for 0% -> 0%
where the time goes in v1:
time: 83.3 us; the launch traced here: 83 us
  Pallas kernels  75.2 us (90%)
  local copies, waits for them, and re-layouts  7.17 us (9%)
    pallas_call x1, Pallas kernels, shards(): pl.pallas_call(kernel, out_shape=[jax.ShapeDtypeStruct((SLOTS, FFW), BF16...  75.2 us
    unnamed x13, local copies, waits for them, and re-layouts  7.17 us

profile of v1, /device:TPU:1, one launch (start us, length us, event | category | flops | bytes accessed | tf_op | source)
XLA Modules:
  0.0 83.0 jit_solution(10113070428418858079)
XLA Ops:
  0.6 0.0 copy-start
  0.6 1.9 %copy-done = bf16[1,768,2048]{2,1,0:T(8,128)(2,1)S(1)} copy-done((bf16[1,768,2048]{2,1,0:T(8,128)(2,1)S(1)}, bf16[1,768,2048]{2,1,0:T(8,128)(2,1)}, u32[]{:S(2)}) %copy-start) | copy-done | bytes 3145752
  2.5 0.0 copy-start.1
  2.5 1.0 %copy-done.1 = bf16[128,2048]{1,0:T(8,128)(2,1)S(1)} copy-done((bf16[128,2048]{1,0:T(8,128)(2,1)S(1)}, bf16[128,2048]{1,0:T(8,128)(2,1)}, u32[]{:S(2)}) %copy-start.1) | copy-done | bytes 524312
  3.6 0.0 copy-start.2
  3.6 1.0 %copy-done.2 = bf16[1,1,192,768]{3,2,1,0:T(8,128)(2,1)S(1)} copy-done((bf16[1,1,192,768]{3,2,1,0:T(8,128)(2,1)S(1)}, bf16[1,1,192,768]{3,2,1,0:T(8,128)(2,1)}, u32[]{:S(2)}) %copy-start.2) | copy-done | bytes 294936
  4.5 0.0 copy-start.3
  4.5 0.7 copy-done.3
  5.2 0.0 copy-start.4
  5.2 0.7 copy-done.4
  5.8 75.2 %shard_map.76 = (bf16[192,768]{1,0:T(8,128)(2,1)S(1)}, f32[128,768]{1,0:T(8,128)S(1)}, f32[1,128]{1,0:T(1,128)S(1)}) custom-call(s32[1,128]{1,0:T(1,128)S(1)} %bitcast.11, bf16[1,128]{1,0:T(2,128)(2,1)S(1)} %bitcast.12, bf16[128,2048]{1,0:T(8,128)(2,1)S(1)} %copy-done.1, bf16[192,768]{1,0:T(8,128)(2,1)S(1)} %bitcast.10, bf16[768,2048]{1,0:T(8,128)(2,1)S(1)} %bitcast.9), custom_call_target="tpu_custom_call" | custom-call | flops 2000000000 | bytes 6000000 | tf_op jit(solution)/shard_map/pallas_call | solution.py:331
  81.0 0.7 copy.11
  81.8 0.7 copy.12
  82.5 0.5 copy.13
Async XLA Ops:
  0.6 1.9 %copy-start = (bf16[1,768,2048]{2,1,0:T(8,128)(2,1)S(1)}, bf16[1,768,2048]{2,1,0:T(8,128)(2,1)}, u32[]{:S(2)}) copy-start(bf16[1,768,2048]{2,1,0:T(8,128)(2,1)} %param.9) | copy-start | bytes 9437188
  2.5 1.0 %copy-start.1 = (bf16[128,2048]{1,0:T(8,128)(2,1)S(1)}, bf16[128,2048]{1,0:T(8,128)(2,1)}, u32[]{:S(2)}) copy-start(bf16[128,2048]{1,0:T(8,128)(2,1)} %grad_hbm.1) | copy-start | bytes 1572868
  3.6 1.0 %copy-start.2 = (bf16[1,1,192,768]{3,2,1,0:T(8,128)(2,1)S(1)}, bf16[1,1,192,768]{3,2,1,0:T(8,128)(2,1)}, u32[]{:S(2)}) copy-start(bf16[1,1,192,768]{3,2,1,0:T(8,128)(2,1)} %param.8) | copy-start | bytes 884740
  4.5 0.7 copy-start.3
  5.2 0.7 copy-start.4

commit v2 on v1

--- a/solution.py
+++ b/solution.py
@@ -16,7 +16,7 @@
 PEERS = NE // CHUNKS
 ROWS = PEERS * CAP
 SLOTS = NE * CAP
-SELF = NE - NX
+SELF = 2 * NX
 TOK = 128
 WIDTH = 2048
 FFW = 768
@@ -27,8 +27,10 @@
 
 def offset_of(o):
     q = o // NX
-    half = (q + 1) // 2
-    return NZ // 2 + half * (1 - 2 * (q % 2)), o % NX
+    j, r = q // 4, q % 4
+    base = jnp.where(r < 2, NZ // 2, jnp.where(r == 3, NZ, 0))
+    dz = base + jnp.where((r == 1) | (r == 2), j, -j)
+    return dz - jnp.where((j == 0) & (r % 2 == 1), NZ // 4, 0), o % NX
 
 
 def target_of(o, z, x):
@@ -56,9 +58,9 @@
 
 
 def kernel(
-    ids_ref, prob_ref, grad_hbm, saved_hbm, weight_hbm,
+    ids_hbm, prob_hbm, grad_hbm, saved_hbm, weight_hbm,
     act_ref, gw_ref, gp_ref,
-    grad, saved, weight, onehot, swap, to_natural,
+    ids_ref, prob_ref, grad, saved, weight, onehot, swap, to_natural,
     send, recv, psend, precv, gsend, grecv,
     arrived, act, wsend, wrecv, gathered,
     load_sem, tok_send, tok_recv, p_send, p_recv, g_send, g_recv,
@@ -70,29 +72,32 @@
     twin = dp + 1 - 2 * core
     right, left = (dp + 2) % NDP, (dp + NDP - 2) % NDP
 
-    barrier = pltpu.get_barrier_semaphore()
-
-    @pl.loop(0, NE)
-    def _(o):
-        @pl.when(o != SELF)
-        def _():
-            pl.semaphore_signal(
-                barrier, inc=1, device_id=(dp, target_of(o, z, x)), device_id_type=MESH
-            )
-
-    @pl.loop(1, NDP)
-    def _(i):
-        pl.semaphore_signal(
-            barrier, inc=1, device_id=((dp + i) % NDP, me), device_id_type=MESH
-        )
-
     loads = [
+        pltpu.make_async_copy(ids_hbm, ids_ref, load_sem.at[3]),
+        pltpu.make_async_copy(prob_hbm, prob_ref, load_sem.at[4]),
         pltpu.make_async_copy(grad_hbm, grad, load_sem.at[0]),
         pltpu.make_async_copy(saved_hbm, saved, load_sem.at[1]),
         pltpu.make_async_copy(weight_hbm, weight, load_sem.at[2]),
     ]
     for load in loads:
         load.start()
+
+    barrier = pltpu.get_barrier_semaphore()
+
+    for dz in (8, 7, 9, 6, 10, 5, 11, 4, 12, 3, 13, 2, 14, 1, 15, 0):
+        for dx in range(NX):
+            if dz or dx:
+                pl.semaphore_signal(
+                    barrier, inc=1, device_id=(dp, ((z + dz) % NZ) * NX + (x + dx) % NX),
+                    device_id_type=MESH,
+                )
+    for i in range(1, NDP):
+        pl.semaphore_signal(
+            barrier, inc=1, device_id=((dp + i) % NDP, me), device_id_type=MESH
+        )
+
+    loads[0].wait()
+    loads[1].wait()
 
     ids = jnp.broadcast_to(ids_ref[...], (TOK, TOK)).astype(F32)
     earlier = lax.broadcasted_iota(jnp.int32, (TOK, TOK), 0) < lax.broadcasted_iota(
@@ -120,7 +125,34 @@
     col = lax.broadcasted_iota(jnp.int32, (256, 256), 1)
     swap[...] = jnp.where(col == 16 * (row % 16) + row // 16, 1.0, 0.0).astype(BF16)
 
-    loads[0].wait()
+    slot_r = lax.broadcasted_iota(jnp.int32, (SLOTS, SLOTS), 0)
+    slot_c = lax.broadcasted_iota(jnp.int32, (SLOTS, SLOTS), 1)
+    peer_r, k_r = slot_parts(slot_r)
+    to_chunk = jnp.where(source_of(peer_r, z, x) * CAP + k_r == slot_c, 1.0, 0.0).astype(BF16)
+    peer_c, k_c = slot_parts(slot_c)
+    to_natural[...] = jnp.where(
+        source_of(peer_c, z, x) * CAP + k_c == slot_r, 1.0, 0.0
+    ).astype(BF16)
+    loads[3].wait()
+    own = dot(to_chunk, saved[...]).astype(BF16)
+    for j in range(CHUNKS):
+        gathered[j, dp] = own[ROWS * j : ROWS * (j + 1)]
+
+    def pass_on(j, r, device, sem):
+        pltpu.make_async_remote_copy(
+            src_ref=gathered.at[j, r], dst_ref=gathered.at[j, r],
+            send_sem=s_send, recv_sem=sem,
+            device_id=(device, me), device_id_type=MESH,
+        ).start()
+
+    def await_piece(j, r, sem):
+        pltpu.make_async_remote_copy(
+            src_ref=gathered.at[j, r], dst_ref=gathered.at[j, r],
+            send_sem=s_send, recv_sem=sem,
+            device_id=(twin, me), device_id_type=MESH,
+        ).wait_recv()
+
+    loads[2].wait()
     for j in range(CHUNKS):
         picked = dot(onehot[ROWS * j : ROWS * (j + 1), :].astype(BF16), grad[...]).astype(BF16)
         for i in range(CAP):
@@ -149,41 +181,15 @@
                     device_id=peer_id, device_id_type=MESH,
                 ).start()
 
+        if j == 0:
+            for i in range(CHUNKS):
+                pass_on(i, dp, right, right_recv.at[0, i])
+                pass_on(i, dp, left, left_recv.at[0, i])
+            for i in range(CHUNKS):
+                pass_on(i, dp, twin, twin_recv)
     recv[SELF] = send[SELF]
     precv[SELF] = psend[SELF]
 
-    slot_r = lax.broadcasted_iota(jnp.int32, (SLOTS, SLOTS), 0)
-    slot_c = lax.broadcasted_iota(jnp.int32, (SLOTS, SLOTS), 1)
-    peer_r, k_r = slot_parts(slot_r)
-    to_chunk = jnp.where(source_of(peer_r, z, x) * CAP + k_r == slot_c, 1.0, 0.0).astype(BF16)
-    peer_c, k_c = slot_parts(slot_c)
-    to_natural[...] = jnp.where(
-        source_of(peer_c, z, x) * CAP + k_c == slot_r, 1.0, 0.0
-    ).astype(BF16)
-    loads[1].wait()
-    own = dot(to_chunk, saved[...]).astype(BF16)
-    for j in range(CHUNKS):
-        gathered[j, dp] = own[ROWS * j : ROWS * (j + 1)]
-
-    def pass_on(j, r, device, sem):
-        pltpu.make_async_remote_copy(
-            src_ref=gathered.at[j, r], dst_ref=gathered.at[j, r],
-            send_sem=s_send, recv_sem=sem,
-            device_id=(device, me), device_id_type=MESH,
-        ).start()
-
-    def await_piece(j, r, sem):
-        pltpu.make_async_remote_copy(
-            src_ref=gathered.at[j, r], dst_ref=gathered.at[j, r],
-            send_sem=s_send, recv_sem=sem,
-            device_id=(twin, me), device_id_type=MESH,
-        ).wait_recv()
-
-    for j in range(CHUNKS):
-        pass_on(j, dp, right, right_recv.at[0, j])
-        pass_on(j, dp, left, left_recv.at[0, j])
-    for j in range(CHUNKS):
-        pass_on(j, dp, twin, twin_recv)
     for hop in range(1, 5):
         from_left, from_right = (dp + NDP - 2 * hop) % NDP, (dp + 2 * hop) % NDP
         for j in range(CHUNKS):
@@ -197,10 +203,10 @@
                 if hop < 3 or (hop == 3 and j >= 2):
                     pass_on(j, from_right, left, left_recv.at[hop, j])
                 pass_on(j, from_right, twin, twin_recv)
-    loads[2].wait()
+    loads[4].wait()
 
     def take(j):
-        count = PEERS - (1 if j == CHUNKS - 1 else 0)
+        count = PEERS - (1 if j == SELF // PEERS else 0)
         pltpu.make_async_remote_copy(
             src_ref=send.at[pl.ds(0, count)], dst_ref=recv.at[pl.ds(0, count)],
             send_sem=tok_send, recv_sem=tok_recv.at[j],
@@ -284,14 +290,14 @@
         send_sem=s_send, recv_sem=twin_recv, device_id=(twin, me), device_id_type=MESH,
     ).wait_recv()
     take(2)
+    back(2)
+    add(0)
     take(3)
-    back(2)
     back(3)
     grecv[SELF] = gsend[SELF]
-    add(0)
     add(1)
+    add(2)
     act_ref[...] = dot(to_natural[...], act[...]).astype(BF16)
-    add(2)
     add(3)
 
     def all_but_one(ref, sem):
@@ -326,7 +332,7 @@
 
 def shards(grad_out, route_prob, expert_ids, saved_act, down_weight):
     vmem = pl.BlockSpec(memory_space=pltpu.VMEM)
-    anywhere = pl.BlockSpec(memory_space=pl.ANY)
+    hbm = pl.BlockSpec(memory_space=pltpu.HBM)
     dma = pltpu.SemaphoreType.DMA
     act, grad_weight, grad_prob = pl.pallas_call(
         kernel,
@@ -335,9 +341,11 @@
             jax.ShapeDtypeStruct((128, FFW), F32),
             jax.ShapeDtypeStruct((1, TOK), F32),
         ],
-        in_specs=[vmem, vmem, anywhere, anywhere, anywhere],
+        in_specs=[hbm] * 5,
         out_specs=[vmem, vmem, vmem],
         scratch_shapes=[
+            pltpu.VMEM((1, TOK), jnp.int32),
+            pltpu.VMEM((1, TOK), BF16),
             pltpu.VMEM((TOK, WIDTH), BF16),
             pltpu.VMEM((SLOTS, FFW), BF16),
             pltpu.VMEM((FFW, WIDTH), BF16),
@@ -355,7 +363,7 @@
             pltpu.VMEM((CHUNKS, NDP, ROWS, 128), BF16),
             pltpu.VMEM((CHUNKS, NDP, ROWS, 128), BF16),
             pltpu.VMEM((CHUNKS, NDP, ROWS, FFW), BF16),
-            dma((3,)),
+            dma((5,)),
             dma, dma((CHUNKS,)),
             dma, dma((CHUNKS,)),
             dma, dma,
@@ -363,7 +371,7 @@
             dma, dma((4, CHUNKS)), dma((4, CHUNKS)), dma,
         ],
         compiler_params=pltpu.CompilerParams(
-            collective_id=0, has_side_effects=True, vmem_limit_bytes=40 << 20
+            collective_id=0, has_side_effects=True, vmem_limit_bytes=60 << 20
         ),
         cost_estimate=pl.CostEstimate(
             flops=2_000_000_000, bytes_accessed=6_000_000, transcendentals=0

time: 83.3 us -> 78 us (0.936)
  Pallas kernels: 75.2 us -> 72.5 us
  local copies, waits for them, and re-layouts: 7.17 us -> 4.58 us
    pallas_call x1, Pallas kernels: 75.2 us -> 72.5 us  [shards(): pl.pallas_call(kernel, out_shape=[jax.ShapeDtypeStruct((SLOTS, FFW), BF16...]
    unnamed x13 -> x3, local copies, waits for them, and re-layouts: 7.17 us -> 4.58 us
where the time goes in v2:
time: 78 us; the launch traced here: 77.7 us
  Pallas kernels  72.5 us (93%)
  local copies, waits for them, and re-layouts  4.58 us (6%)
    pallas_call x1, Pallas kernels, shards(): pl.pallas_call(kernel, out_shape=[jax.ShapeDtypeStruct((SLOTS, FFW), BF16...  72.5 us
    unnamed x3, local copies, waits for them, and re-layouts  4.58 us

profile of v2, /device:TPU:1, one launch (start us, length us, event | category | flops | bytes accessed | tf_op | source)
XLA Modules:
  0.0 77.7 jit_solution(11823098519043222830)
XLA Ops:
  0.6 72.5 %shard_map.76 = (bf16[192,768]{1,0:T(8,128)(2,1)}, f32[128,768]{1,0:T(8,128)}, f32[1,128]{1,0:T(1,128)}) custom-call(s32[1,128]{1,0:T(1,128)} %bitcast.11, bf16[1,128]{1,0:T(2,128)(2,1)} %bitcast.12, bf16[128,2048]{1,0:T(8,128)(2,1)} %grad_hbm.1, bf16[192,768]{1,0:T(8,128)(2,1)} %bitcast.10, bf16[768,2048]{1,0:T(8,128)(2,1)} %bitcast.9), custom_call_target="tpu_custom_call" | custom-call | flops 2000000000 | bytes 6000000 | tf_op jit(solution)/shard_map/pallas_call | solution.py:337
  73.1 1.7 %copy.11 = bf16[1,1,192,768]{3,2,1,0:T(8,128)(2,1)} copy(bf16[1,1,192,768]{3,2,1,0:T(8,128)(2,1)} %bitcast.8) | data formatting | bytes 589824
  74.8 1.8 %copy.12 = f32[1,128,768]{2,1,0:T(8,128)} copy(f32[1,128,768]{2,1,0:T(8,128)} %bitcast.7) | data formatting | bytes 786432
  76.6 1.1 %copy.13 = f32[128,1]{0,1:T(1,128)} copy(f32[128,1]{0,1:T(1,128)} %bitcast.13) | data formatting | bytes 1024
